TPU v7x, 256 devices: a whole 4x4x8 slice. The times are simulated.
256 devices in a mesh: ctx: 32 (over y, z_lo, x), exp: 8 (over z_hi, core).
Axes of the slice: x: 4, y: 4, z: 8 (z_hi: 4, z_lo: 2; z = z_hi * 2 + z_lo), core: 2. Of those that a mesh axis runs over, the one named last changes fastest.
Arguments:
- lin_query: bfloat16 [4096, 8192], P('ctx', 'exp'), may hold values from -5 to 5
- lin_key: bfloat16 [4096, 8192], P('ctx', 'exp'), may hold values from -5 to 5
- lin_value: bfloat16 [4096, 8192], P('ctx', 'exp'), may hold values from -5 to 5
- log_decay: float32 [4096, 64], P('ctx', 'exp'), may hold values from -1.5 to 0
- lin_gain: float32 [8192], P('exp'), may hold values from 0.25 to 1.75
- moe_input: bfloat16 [1536, 6144], P(('ctx', 'exp')), may hold values from -6 to 6
- routes: int32 [1536, 2], P(('ctx', 'exp')), may hold values from 0 to 7, all different within a row; in each aligned block of 6 rows (0 to 5, 6 to 11, ...) at most 2 rows name the same one
- route_weight: float32 [1536, 2], P(('ctx', 'exp')), may hold values from 0.2 to 1
- gate_weight: bfloat16 [8, 6144, 9216], P('exp', None, 'ctx'), may hold values from -0.078125 to 0.078125
- up_weight: bfloat16 [8, 6144, 9216], P('exp', None, 'ctx'), may hold values from -0.078125 to 0.078125
- down_weight: bfloat16 [8, 9216, 6144], P('exp', 'ctx'), may hold values from -0.0625 to 0.0625
- soft_query: bfloat16 [4096, 8192], P('ctx', 'exp'), may hold values from -5 to 5
- soft_kv: bfloat16 [4096, 8, 2, 128], P('ctx', 'exp'), may hold values from -5 to 5
Outputs:
- lin_out: bfloat16 [4096, 8192], P('ctx', 'exp')
- moe_out: bfloat16 [1536, 6144], P(('ctx', 'exp'))
- soft_out: bfloat16 [4096, 8192], P('ctx', 'exp')
Inputs may be any that keep to these rules, and one draw needn't show every extreme that they name: `routes`: within the rows of one device (6 rows) each expert is named by at most 2 of them; the 2 experts of a row differ.
All inputs are finite; a program needn't handle non-finite values.
Results may differ from a plain program's by a relative error of at most 0.009.
Values may be sent and summed in bfloat16 or wider, within the bound.
A program may use at most 128 MiB of HBM per device.

v0:
```python
import math
import jax
import jax.numpy as jnp
from jax import lax
from jax.sharding import PartitionSpec as P

D = 6144
HEAD_TOTAL = 64
HEAD = 128
KV_HEADS = 8
EXPERTS = 8
TOP = 2
CAP = 2


def prefix(value, axis, join, neutral):
    count, mine = (lax.axis_size(axis), lax.axis_index(axis))
    pieces = jax.tree.map(lambda part: lax.all_gather(part, axis), value)
    so_far = jax.tree.map(
        lambda part, zero: jnp.full_like(part, 0) + jnp.asarray(zero, part.dtype), value, neutral
    )

    def hop(position, so_far):
        longer = join(so_far, jax.tree.map(lambda part: part[position], pieces))
        return jax.tree.map(lambda new, old: jnp.where(position < mine, new, old), longer, so_far)

    return lax.fori_loop(0, count - 1, hop, so_far)


def lightning(lin_query, lin_key, lin_value, log_decay, lin_gain):
    length = lin_query.shape[0]
    heads_here = log_decay.shape[1]
    score_scale = 1.0 / math.sqrt(HEAD)
    queries = lin_query.reshape(length, heads_here, HEAD)
    key_rows = lin_key.reshape(length, heads_here, HEAD)
    value_f = lin_value.reshape(length, heads_here, HEAD).astype(jnp.float32)
    cumulative = jnp.cumsum(log_decay, axis=0)
    scores = (
        jnp.einsum("thd,jhd->htj", queries, key_rows, preferred_element_type=jnp.float32)
        * score_scale
    )
    spread = cumulative.T[:, :, None] - cumulative.T[:, None, :]
    causal = jnp.tril(jnp.ones((length, length), dtype=jnp.bool_))
    decays = jnp.where(causal[None], jnp.exp(jnp.where(causal[None], spread, 0.0)), 0.0)
    within = jnp.einsum("htj,jhd->thd", scores * decays, value_f, precision=lax.Precision.HIGHEST)
    tail_decay = jnp.exp(cumulative[-1][None, :] - cumulative)
    local_state = jnp.einsum(
        "th,thd,the->hde",
        tail_decay,
        key_rows.astype(jnp.float32),
        value_f,
        precision=lax.Precision.HIGHEST,
    )

    def combine(earlier, latter):
        return (earlier[0] + latter[0], jnp.exp(latter[0])[:, None, None] * earlier[1] + latter[1])

    identity = (
        jnp.zeros((heads_here,), jnp.float32),
        jnp.zeros((heads_here, HEAD, HEAD), jnp.float32),
    )
    prior_log, prior_state = prefix((cumulative[-1], local_state), "ctx", combine, identity)
    carried = (
        jnp.exp(cumulative)[:, :, None]
        * jnp.einsum(
            "thd,hde->the",
            queries.astype(jnp.float32),
            prior_state,
            precision=lax.Precision.HIGHEST,
        )
        * score_scale
    )
    combined = within + carried
    root_mean = jnp.sqrt(jnp.mean(combined * combined, axis=-1, keepdims=True) + 1e-06)
    normed = combined / root_mean * lin_gain.reshape(heads_here, HEAD)
    return normed.reshape(length, heads_here * HEAD).astype(jnp.bfloat16)


def experts_layer(moe_input, routes, route_weight, gate_weight, up_weight, down_weight):
    row_count = moe_input.shape[0]
    pair_count = row_count * TOP
    flat_ids = routes.reshape(pair_count)
    same_expert = flat_ids[:, None] == flat_ids[None, :]
    pair_order = jnp.arange(pair_count, dtype=jnp.int32)
    earlier_pair = pair_order[None, :] < pair_order[:, None]
    slot_rank = jnp.sum(jnp.logical_and(same_expert, earlier_pair), axis=1)
    slot_index = slot_rank * EXPERTS + flat_ids
    onehot = (slot_index[None, :] == jnp.arange(CAP * EXPERTS, dtype=jnp.int32)[:, None]).astype(
        jnp.bfloat16
    )
    pair_rows = jnp.repeat(moe_input, TOP, axis=0)
    outgoing = (
        jnp.dot(onehot, pair_rows, preferred_element_type=jnp.float32)
        .astype(jnp.bfloat16)
        .reshape(CAP, EXPERTS, D)
    )
    arrived = lax.all_to_all(outgoing, "exp", split_axis=1, concat_axis=0, tiled=True)
    shard_piece = lax.all_gather(arrived, "ctx", axis=0, tiled=True)
    gate_part = jnp.einsum(
        "red,edf->ref", shard_piece, gate_weight, preferred_element_type=jnp.float32
    )
    up_part = jnp.einsum("red,edf->ref", shard_piece, up_weight, preferred_element_type=jnp.float32)
    hidden = (jax.nn.silu(gate_part) * up_part).astype(jnp.bfloat16)
    expert_out = lax.psum_scatter(
        jnp.einsum("ref,efd->red", hidden, down_weight, preferred_element_type=jnp.float32),
        "ctx",
        scatter_dimension=0,
        tiled=True,
    ).astype(jnp.bfloat16)
    returned = lax.all_to_all(expert_out, "exp", split_axis=0, concat_axis=1, tiled=True).reshape(
        CAP * EXPERTS, D
    )
    pair_out = jnp.dot(onehot.T, returned, preferred_element_type=jnp.float32).reshape(
        row_count, TOP, D
    )
    mixed = jnp.sum(pair_out * route_weight[:, :, None], axis=1)
    return mixed.astype(jnp.bfloat16)


def softmax_layer(soft_query, soft_kv):
    length = soft_query.shape[0]
    kv_here = soft_kv.shape[1]
    group = HEAD_TOTAL // KV_HEADS
    score_scale = 1.0 / math.sqrt(HEAD)
    queries = soft_query.reshape(length, kv_here, group, HEAD)
    query_pos = lax.axis_index("ctx") * length + jnp.arange(length, dtype=jnp.int32)
    shard_piece = lax.all_gather(soft_kv, "ctx", axis=0, tiled=True)
    maxima = jnp.full((kv_here, group, length), -jnp.inf, jnp.float32)
    totals = jnp.zeros((kv_here, group, length), jnp.float32)
    running = jnp.zeros((kv_here, group, length, HEAD), jnp.float32)
    key_rows = shard_piece[:, :, 0, :]
    value_rows = shard_piece[:, :, 1, :]
    key_pos = jnp.arange(shard_piece.shape[0], dtype=jnp.int32)
    scores = (
        jnp.einsum("tghd,jgd->ghtj", queries, key_rows, preferred_element_type=jnp.float32)
        * score_scale
    )
    allowed = key_pos[None, :] <= query_pos[:, None]
    scores = jnp.where(allowed[None, None], scores, -jnp.inf)
    new_max = jnp.max(scores, axis=-1)
    safe_max = jnp.where(jnp.isfinite(new_max), new_max, 0.0)
    shrink = jnp.exp(maxima - safe_max)
    weights = jnp.exp(scores - safe_max[..., None])
    totals = totals * shrink + jnp.sum(weights, axis=-1)
    update = jnp.einsum(
        "ghtj,jgd->ghtd",
        weights.astype(jnp.bfloat16),
        value_rows,
        preferred_element_type=jnp.float32,
    )
    running = running * shrink[..., None] + update
    output = running / totals[..., None]
    return output.transpose(2, 0, 1, 3).reshape(length, kv_here * group * HEAD).astype(jnp.bfloat16)


def on_device(
    lin_query,
    lin_key,
    lin_value,
    log_decay,
    lin_gain,
    moe_input,
    routes,
    route_weight,
    gate_weight,
    up_weight,
    down_weight,
    soft_query,
    soft_kv,
):
    lin_out = lightning(lin_query, lin_key, lin_value, log_decay, lin_gain)
    soft_out = softmax_layer(soft_query, soft_kv)
    moe_out = experts_layer(moe_input, routes, route_weight, gate_weight, up_weight, down_weight)
    return (lin_out, moe_out, soft_out)


def solution(mesh):
    placed = (
        P("ctx", "exp"),
        P("ctx", "exp"),
        P("ctx", "exp"),
        P("ctx", "exp"),
        P("exp"),
        P(("ctx", "exp"), None),
        P(("ctx", "exp"), None),
        P(("ctx", "exp"), None),
        P("exp", None, "ctx"),
        P("exp", None, "ctx"),
        P("exp", "ctx", None),
        P("ctx", "exp"),
        P("ctx", "exp", None, None),
    )
    return jax.shard_map(
        on_device,
        mesh=mesh,
        in_specs=placed,
        out_specs=(P("ctx", "exp"), P(("ctx", "exp"), None), P("ctx", "exp")),
        check_vma=False,
    )
```

profile of v0, /device:TPU:1, one launch (start us, length us, event | category | flops | bytes accessed | tf_op | source)
XLA Modules:
  0.0 780.1 jit_solution(14892325670164838628)
XLA Ops:
  13.0 18.5 %all_to_all.33 = bf16[2,8,6144]{2,0,1:T(2,128)(2,1)} all-to-all(bf16[2,8,6144]{2,0,1:T(2,128)(2,1)S(1)} %copy.120), channel_id=1, replica_groups=mesh['ctx'=32,'exp'=8] {'exp'}, dimensions={1} | all-to-all | bytes 393216 | tf_op jit(solution)/shard_map/all_to_all | solution.py:97
  43.3 2.2 fusion.56
  45.6 132.8 %all-gather.6.cloned.1.call-done = bf16[512,1,6144]{2,0,1:T(8,128)(2,1)} async-done(((bf16[16,1,6144]{2,0,1:T(8,128)(2,1)}), bf16[512,1,6144]{2,0,1:T(8,128)(2,1)}) %all-gather.6.cloned.1.call-update) | async-done | bytes 6291472 | tf_op jit(solution)/shard_map/all_gather | solution.py:98
  178.4 6.0 fusion.16
  187.1 6.4 convolution_bitcast_fusion
  194.6 68.3 %all-gather.1 = f32[32,1,8]{2,1,0:T(1,128)} all-gather(f32[1,1,8]{2,1,0:T(1,128)S(1)} %copy-done.7), channel_id=1, replica_groups=mesh['ctx'=32,'exp'=8] {'ctx'}, dimensions={0}, use_global_device_ids=true | all-gather | bytes 1056 | tf_op jit(solution)/shard_map/all_gather | solution.py:18
  264.4 69.8 %all-gather.8.cloned.1.call-done = bf16[4096,1,2,128]{3,0,2,1:T(8,128)(2,1)} async-done(((bf16[128,1,2,128]{3,0,2,1:T(8,128)(2,1)}), bf16[4096,1,2,128]{3,0,2,1:T(8,128)(2,1)}) %all-gather.8.cloned.1.call-update) | async-done | bytes 2097168 | tf_op jit(solution)/shard_map/all_gather | solution.py:127
  334.2 8.2 %fusion.3 = (f32[8,128]{1,0:T(8,128)S(1)}, f32[4096,128,8]{1,0,2:T(8,128)}) fusion(pred[128,4096]{0,1:T(8,128)(4,1)S(1)} %iota_compare_fusion, bf16[4096,1,2,128]{3,0,2,1:T(8,128)(2,1)} %all-gather.8.cloned.1.call-done, bf16[128,1024]{1,0:T(8,128)(2,1)S(1)} %copy-done.11), kind=kOutput, calls=%fused_computation.7 | convolution fusion | flops 1086323712 | bytes 18616320 | tf_op jit(solution)/shard_map/tghd,jgd->ghtj/dot_general | solution.py:135
  342.4 9.3 %fusion.1 = f32[8,128]{1,0:T(8,128)S(1)} fusion(f32[4096,128,8]{1,0,2:T(8,128)} %get-tuple-element.152, f32[8,128]{1,0:T(8,128)S(1)} %is-finite_select_fusion, pred[128,4096]{0,1:T(8,128)(4,1)S(1)} %iota_compare_fusion), kind=kLoop, calls=%fused_computation.5 | loop fusion | flops 16776192 | bytes 17309696 | tf_op jit(solution)/shard_map/reduce_sum | solution.py:144
  351.8 8.6 %fusion.53 = bf16[8,128,128]{1,2,0:T(8,128)(2,1)} fusion(bf16[4096,1,2,128]{3,0,2,1:T(8,128)(2,1)S(1)} %copy-done.10, f32[4096,128,8]{1,0,2:T(8,128)} %get-tuple-element.152, f32[8,128]{1,0:T(8,128)S(1)} %is-finite_select_fusion, pred[128,4096]{0,1:T(8,128)(4,1)S(1)} %iota_compare_fusion, f32[8,128]{1,0:T(8,128)S(1)} %get-tuple-element.146, ...), kind=kOutput, calls=%fused_computation.41 | convolution fusion | flops 1090912256 | bytes 18624512 | tf_op jit(solution)/shard_map/ghtj,jgd->ghtd/dot_general | solution.py:145
  362.3 183.9 %all-gather.10.cloned.1.call-done = f32[256,128,128]{2,1,0:T(8,128)} async-done(((f32[8,128,128]{2,1,0:T(8,128)}), f32[256,128,128]{2,1,0:T(8,128)}) %all-gather.10.cloned.1.call-update) | async-done | bytes 16777232 | tf_op jit(solution)/shard_map/all_gather | solution.py:18
  546.2 87.4 %while.14 = (s32[]{:T(128)}, f32[8,128,128]{2,1,0:T(8,128)}, s32[]{:T(128)}, f32[32,8]{1,0:T(8,128)}, f32[32,8,128,128]{3,2,1,0:T(8,128)}, /*index=5*/s32[]{:T(128)}, s32[]{:T(128)}) while((s32[]{:T(128)}, f32[8,128,128]{2,1,0:T(8,128)}, s32[]{:T(128)}, f32[32,8]{1,0:T(8,128)}, f32[32,8,128,128]{3,2,1,0:T(8,128)}, ...), condition=%wide.region_2.3_spmd.clone, body=%wide.region_1.2_spmd.clone.sunk | while | flops 524292 | bytes 1573065 | solution.py:27
  563.6 2.1 fusion.93
  572.1 2.1 fusion.93
  575.0 2.1 fusion.93
  589.1 2.1 fusion.93
  591.9 2.1 fusion.93
  597.6 2.1 fusion.93
  600.4 2.1 fusion.93
  611.7 2.1 fusion.93
  614.5 2.1 fusion.93
  623.0 2.1 fusion.93
  625.8 2.1 fusion.93
  628.6 2.1 fusion.93
  631.4 2.1 fusion.93
  635.3 2.6 multiply_reduce_fusion
  637.9 84.6 %reduce-scatter.2.cloned.1.call-done = f32[16,1,6144]{2,0,1:T(8,128)} async-done(((f32[512,1,6144]{2,0,1:T(8,128)}), f32[16,1,6144]{2,0,1:T(8,128)}) %reduce-scatter.2.cloned.1.call-update) | async-done | bytes 393232 | tf_op jit(solution)/shard_map/reduce_scatter | solution.py:104
  724.7 2.3 reduce.3
  728.8 27.5 %all-to-all-start.1 = ((bf16[8,2,6144]{2,1,0:T(2,128)(2,1)}), bf16[8,2,6144]{2,1,0:T(2,128)(2,1)}, u32[]{:S(2)}, u32[]{:S(2)}) async-start(bf16[8,2,6144]{2,1,0:T(2,128)(2,1)} %reshape.218), calls=%async_computation.2 | async-start | bytes 393216 | tf_op jit(solution)/shard_map/all_to_all | solution.py:110
  760.0 5.0 all-to-all-done.1
  764.9 2.2 reshape.219
  767.2 2.8 reduce.2
  (120 shorter events, 97.3 us)
Async XLA Ops:
  7.2 179.9 %copy-start = (bf16[1,288,6144]{2,1,0:T(8,128)(2,1)S(1)}, bf16[1,288,6144]{2,1,0:T(8,128)(2,1)}, u32[]{:S(2)}) copy-start(bf16[1,288,6144]{2,1,0:T(8,128)(2,1)} %param.25) | copy-start | bytes 10616836
  7.2 171.2 %all-gather.6.cloned.1.call-start = ((), (), s32[]{:S(2)}) async-start(), calls=%async_computation.3 | async-start | bytes 6488064 | tf_op jit(solution)/shard_map/all_gather | solution.py:98
  33.3 301.0 %all-gather.8.cloned.1.call-start = ((), (), s32[]{:S(2)}) async-start(), calls=%async_computation.5 | async-start | bytes 2162688 | tf_op jit(solution)/shard_map/all_gather | solution.py:127
  34.8 511.4 %all-gather.10.cloned.1.call-start = ((), (), s32[]{:S(2)}) async-start(), calls=%async_computation.6 | async-start | bytes 17301504 | tf_op jit(solution)/shard_map/all_gather | solution.py:18
  45.6 676.9 %reduce-scatter.2.cloned.1.call-start = ((), (), s32[]{:S(2)}) async-start(), calls=%async_computation.4 | async-start | bytes 12976128 | tf_op jit(solution)/shard_map/reduce_scatter | solution.py:104
  178.4 6.0 copy-start.8
  178.4 6.6 copy-start.9
  193.5 0.8 copy-start.5
  193.5 0.9 copy-start.3
  193.5 1.1 copy-start.7
  193.5 69.5 %copy-start.2 = (bf16[128,1024]{0,1:T(8,128)(2,1)S(1)}, bf16[128,1024]{0,1:T(8,128)(2,1)}, u32[]{:S(2)}) copy-start(bf16[128,1024]{0,1:T(8,128)(2,1)} %copy.134) | copy-start | bytes 786436
  193.5 69.5 %copy-start.4 = (bf16[128,1024]{1,0:T(8,128)(2,1)S(1)}, bf16[128,1024]{1,0:T(8,128)(2,1)}, u32[]{:S(2)}) copy-start(bf16[128,1024]{1,0:T(8,128)(2,1)} %param.15) | copy-start | bytes 786436
  193.5 140.7 %copy-start.11 = (bf16[128,1024]{1,0:T(8,128)(2,1)S(1)}, bf16[128,1024]{1,0:T(8,128)(2,1)}, u32[]{:S(2)}) copy-start(bf16[128,1024]{1,0:T(8,128)(2,1)} %param.26) | copy-start | bytes 786436
  342.4 9.3 %copy-start.10 = (bf16[4096,1,2,128]{3,0,2,1:T(8,128)(2,1)S(1)}, bf16[4096,1,2,128]{3,0,2,1:T(8,128)(2,1)}, u32[]{:S(2)}) copy-start(bf16[4096,1,2,128]{3,0,2,1:T(8,128)(2,1)} %all-gather.8.cloned.1.call-done) | copy-start | bytes 6291460
  360.3 395.9 %copy-start.6 = (f32[1024]{0:T(1024)S(1)}, f32[1024]{0:T(1024)}, u32[]{:S(2)}) copy-start(f32[1024]{0:T(1024)} %param.19) | copy-start | bytes 12292
  360.3 413.2 %copy-start.1 = (bf16[1,288,6144]{2,1,0:T(8,128)(2,1)S(1)}, bf16[1,288,6144]{2,1,0:T(8,128)(2,1)}, u32[]{:S(2)}) copy-start(bf16[1,288,6144]{2,1,0:T(8,128)(2,1)} %param.25) | copy-start | bytes 10616836
  728.8 36.2 %all-to-all-start.1 = ((bf16[8,2,6144]{2,1,0:T(2,128)(2,1)}), bf16[8,2,6144]{2,1,0:T(2,128)(2,1)}, u32[]{:S(2)}, u32[]{:S(2)}) async-start(bf16[8,2,6144]{2,1,0:T(2,128)(2,1)} %reshape.218), calls=%async_computation.2 | async-start | bytes 393216 | tf_op jit(solution)/shard_map/all_to_all | solution.py:110
Sparse Core Ops, SparseCore 0:
  33.4 144.9 all-gather.5
  180.2 153.9 all-gather.7
  336.0 210.1 all-gather.9
  548.6 173.8 reduce-scatter.1
where the time goes:
time: 783 us; the launch traced here: 780 us
  waiting for transfers between devices  476 us (61%)
  other arithmetic  87.9 us (11%)
  blocking collectives  86.9 us (11%)
  local copies, waits for them, and re-layouts  45.9 us (6%)
  matrix products  41.8 us (5%)
  starting transfers between devices  27.6 us (4%)
  between operations  13.9 us (2%)
    all_gather x1, waiting for transfers between devices, prefix(): pieces = jax.tree.map(lambda part: lax.all_gather(part, axis), value)  184 us
    all_gather x1, waiting for transfers between devices, experts_layer(): shard_piece = lax.all_gather(arrived, 'ctx', axis=0, tiled=True)  133 us
    reduce_scatter x1, waiting for transfers between devices, experts_layer(): lax.psum_scatter(jnp.einsum('ref,efd->red', hidden, down_weight, preferre...  84.6 us
    all_gather x1, waiting for transfers between devices, softmax_layer(): shard_piece = lax.all_gather(soft_kv, 'ctx', axis=0, tiled=True)  69.8 us
    all_gather x1, blocking collectives, prefix(): pieces = jax.tree.map(lambda part: lax.all_gather(part, axis), value)  68.3 us
    select_n x31, other arithmetic, hop(): jnp.where(position < mine, new, old)  66.2 us
    all_to_all x1, starting transfers between devices, experts_layer(): lax.all_to_all(expert_out, 'exp', split_axis=0, concat_axis=1, tiled=True)  27.5 us
    exp x31, local copies, waits for them, and re-layouts, combine(): jnp.exp(latter[0])[:, None, None] * earlier[1] + latter[1]  21.2 us
  transfers between devices with their start and end apart: 5, of which 5 were waited for; matrix products, arithmetic and copies ran while one was open for 19% of the time, Pallas kernels for 0%

commit v1 on v0

--- a/solution.py
+++ b/solution.py
@@ -124,7 +124,9 @@
     score_scale = 1.0 / math.sqrt(HEAD)
     queries = soft_query.reshape(length, kv_here, group, HEAD)
     query_pos = lax.axis_index("ctx") * length + jnp.arange(length, dtype=jnp.int32)
-    shard_piece = lax.all_gather(soft_kv, "ctx", axis=0, tiled=True)
+    reached = jnp.stack([soft_kv for _ in range(lax.axis_size("ctx"))], 0)
+    tile_out = lax.all_to_all(reached, "ctx", split_axis=0, concat_axis=0)
+    shard_piece = jnp.concatenate(tile_out, axis=0)
     maxima = jnp.full((kv_here, group, length), -jnp.inf, jnp.float32)
     totals = jnp.zeros((kv_here, group, length), jnp.float32)
     running = jnp.zeros((kv_here, group, length, HEAD), jnp.float32)

time: 783 us -> 644 us (0.82)
  waiting for transfers between devices: 476 us -> 306 us
  blocking collectives: 86.9 us -> 112 us
    all_gather x1, waiting for transfers between devices: 184 us -> 88.1 us  [prefix(): pieces = jax.tree.map(lambda part: lax.all_gather(part, axis), value)]
    all_gather x1 -> x0, waiting for transfers between devices: 69.8 us -> none  [softmax_layer(): shard_piece = lax.all_gather(soft_kv, 'ctx', axis=0, tiled=True)]
    all_gather x1, blocking collectives: 68.3 us -> 93.3 us  [prefix(): pieces = jax.tree.map(lambda part: lax.all_gather(part, axis), value)]
  transfers between devices with their start and end apart: 5 -> 5, of which waited for: 5 -> 4; matrix products, arithmetic and copies ran while one was open for 19% -> 23% of each run, Pallas kernels for 0% -> 0%
where the time goes in v1:
time: 644 us; the launch traced here: 641 us
  waiting for transfers between devices  306 us (48%)
  blocking collectives  112 us (17%)
  other arithmetic  88.7 us (14%)
  local copies, waits for them, and re-layouts  45.5 us (7%)
  matrix products  40.1 us (6%)
  starting transfers between devices  34.5 us (5%)
  between operations  14 us (2%)
    all_gather x1, waiting for transfers between devices, experts_layer(): shard_piece = lax.all_gather(arrived, 'ctx', axis=0, tiled=True)  134 us
    all_gather x1, blocking collectives, prefix(): pieces = jax.tree.map(lambda part: lax.all_gather(part, axis), value)  93.3 us
    all_gather x1, waiting for transfers between devices, prefix(): pieces = jax.tree.map(lambda part: lax.all_gather(part, axis), value)  88.1 us
    reduce_scatter x1, waiting for transfers between devices, experts_layer(): lax.psum_scatter(jnp.einsum('ref,efd->red', hidden, down_weight, preferre...  78.8 us
    select_n x31, other arithmetic, hop(): jnp.where(position < mine, new, old)  66.8 us
    all_to_all x1, starting transfers between devices, experts_layer(): lax.all_to_all(expert_out, 'exp', split_axis=0, concat_axis=1, tiled=True)  28.6 us
    exp x31, local copies, waits for them, and re-layouts, combine(): jnp.exp(latter[0])[:, None, None] * earlier[1] + latter[1]  21.4 us
    all_to_all x1, blocking collectives, experts_layer(): lax.all_to_all(outgoing, 'exp', split_axis=1, concat_axis=0, tiled=True)  18.5 us
  transfers between devices with their start and end apart: 5, of which 4 were waited for; matrix products, arithmetic and copies ran while one was open for 23% of the time, Pallas kernels for 0%

profile of v1, /device:TPU:1, one launch (start us, length us, event | category | flops | bytes accessed | tf_op | source)
XLA Modules:
  0.0 641.0 jit_solution(9464602623129970421)
XLA Ops:
  13.0 18.5 %all_to_all.38 = bf16[2,8,6144]{2,0,1:T(2,128)(2,1)} all-to-all(bf16[2,8,6144]{2,0,1:T(2,128)(2,1)S(1)} %copy.122), channel_id=1, replica_groups=mesh['ctx'=32,'exp'=8] {'exp'}, dimensions={1} | all-to-all | bytes 393216 | tf_op jit(solution)/shard_map/all_to_all | solution.py:97
  41.8 2.3 fusion.56
  44.1 134.3 %all-gather.5.cloned.1.call-done = bf16[512,1,6144]{2,0,1:T(8,128)(2,1)} async-done(((bf16[16,1,6144]{2,0,1:T(8,128)(2,1)}), bf16[512,1,6144]{2,0,1:T(8,128)(2,1)}) %all-gather.5.cloned.1.call-update) | async-done | bytes 6291472 | tf_op jit(solution)/shard_map/all_gather | solution.py:98
  178.4 6.0 fusion.16
  187.1 6.3 convolution_bitcast_fusion
  196.2 5.7 all-to-all-start.2
  202.2 93.3 %all-gather.1 = f32[32,1,8]{2,1,0:T(1,128)} all-gather(f32[1,1,8]{2,1,0:T(1,128)S(1)} %copy-done.10), channel_id=1, replica_groups=mesh['ctx'=32,'exp'=8] {'ctx'}, dimensions={0}, use_global_device_ids=true | all-gather | bytes 1056 | tf_op jit(solution)/shard_map/all_gather | solution.py:18
  297.2 7.1 %fusion.3 = (f32[8,128]{1,0:T(8,128)S(1)}, f32[4096,128,8]{1,0,2:T(8,128)}) fusion(pred[128,4096]{0,1:T(8,128)(4,1)S(1)} %iota_compare_fusion, bf16[4096,1,2,128]{3,0,2,1:T(8,128)(2,1)S(1)} %bitcast.197, bf16[128,1024]{1,0:T(8,128)(2,1)S(1)} %copy-done.13), kind=kOutput, calls=%fused_computation.7 | convolution fusion | flops 1086323712 | bytes 18616320 | tf_op jit(solution)/shard_map/tghd,jgd->ghtj/dot_general | solution.py:137
  304.4 9.5 %fusion.1 = f32[8,128]{1,0:T(8,128)S(1)} fusion(f32[4096,128,8]{1,0,2:T(8,128)} %get-tuple-element.152, f32[8,128]{1,0:T(8,128)S(1)} %is-finite_select_fusion, pred[128,4096]{0,1:T(8,128)(4,1)S(1)} %iota_compare_fusion), kind=kLoop, calls=%fused_computation.5 | loop fusion | flops 16776192 | bytes 17309696 | tf_op jit(solution)/shard_map/reduce_sum | solution.py:146
  313.8 8.0 %fusion.53 = bf16[8,128,128]{1,2,0:T(8,128)(2,1)S(1)} fusion(bf16[4096,1,2,128]{3,0,2,1:T(8,128)(2,1)S(1)} %bitcast.198, f32[4096,128,8]{1,0,2:T(8,128)} %get-tuple-element.152, f32[8,128]{1,0:T(8,128)S(1)} %is-finite_select_fusion, pred[128,4096]{0,1:T(8,128)(4,1)S(1)} %iota_compare_fusion, f32[8,128]{1,0:T(8,128)S(1)} %get-tuple-element.146, ...), kind=kOutput, calls=%fused_computation.41 | convolution fusion | flops 1090912256 | bytes 18624512 | tf_op jit(solution)/shard_map/ghtj,jgd->ghtd/dot_general | solution.py:147
  322.7 88.1 %all-gather.7.cloned.1.call-done = f32[256,128,128]{2,1,0:T(8,128)} async-done(((f32[8,128,128]{2,1,0:T(8,128)}), f32[256,128,128]{2,1,0:T(8,128)}) %all-gather.7.cloned.1.call-update) | async-done | bytes 16777232 | tf_op jit(solution)/shard_map/all_gather | solution.py:18
  410.8 88.2 %while.14 = (s32[]{:T(128)}, f32[8,128,128]{2,1,0:T(8,128)}, s32[]{:T(128)}, f32[32,8]{1,0:T(8,128)}, f32[32,8,128,128]{3,2,1,0:T(8,128)}, /*index=5*/s32[]{:T(128)}, s32[]{:T(128)}) while((s32[]{:T(128)}, f32[8,128,128]{2,1,0:T(8,128)}, s32[]{:T(128)}, f32[32,8]{1,0:T(8,128)}, f32[32,8,128,128]{3,2,1,0:T(8,128)}, ...), condition=%wide.region_2.3_spmd.clone, body=%wide.region_1.2_spmd.clone.sunk | while | flops 524292 | bytes 1573065 | solution.py:27
  411.7 2.2 fusion.93
  434.4 2.2 fusion.93
  437.3 2.2 fusion.93
  443.0 2.2 fusion.93
  445.8 2.2 fusion.93
  448.7 2.2 fusion.93
  451.5 2.2 fusion.93
  454.4 2.2 fusion.93
  465.7 2.2 fusion.93
  479.9 2.2 fusion.93
  482.7 2.2 fusion.93
  485.5 2.2 fusion.93
  488.4 2.2 fusion.93
  500.7 2.6 multiply_reduce_fusion
  503.4 78.8 %reduce-scatter.2.cloned.1.call-done = f32[16,1,6144]{2,0,1:T(8,128)} async-done(((f32[512,1,6144]{2,0,1:T(8,128)}), f32[16,1,6144]{2,0,1:T(8,128)}) %reduce-scatter.2.cloned.1.call-update) | async-done | bytes 393232 | tf_op jit(solution)/shard_map/reduce_scatter | solution.py:104
  584.4 2.3 reduce.3
  588.5 28.6 %all-to-all-start.1 = ((bf16[8,2,6144]{2,1,0:T(2,128)(2,1)}), bf16[8,2,6144]{2,1,0:T(2,128)(2,1)}, u32[]{:S(2)}, u32[]{:S(2)}) async-start(bf16[8,2,6144]{2,1,0:T(2,128)(2,1)} %reshape.225), calls=%async_computation.2 | async-start | bytes 393216 | tf_op jit(solution)/shard_map/all_to_all | solution.py:110
  620.9 5.0 all-to-all-done.1
  625.9 2.2 reshape.226
  628.1 2.8 reduce.2
  (125 shorter events, 97.2 us)
Async XLA Ops:
  7.2 179.9 %copy-start = (bf16[1,288,6144]{2,1,0:T(8,128)(2,1)S(1)}, bf16[1,288,6144]{2,1,0:T(8,128)(2,1)}, u32[]{:S(2)}) copy-start(bf16[1,288,6144]{2,1,0:T(8,128)(2,1)} %param.25) | copy-start | bytes 10616836
  7.2 171.2 %all-gather.5.cloned.1.call-start = ((), (), s32[]{:S(2)}) async-start(), calls=%async_computation.4 | async-start | bytes 6488064 | tf_op jit(solution)/shard_map/all_gather | solution.py:98
  33.3 377.6 %all-gather.7.cloned.1.call-start = ((), (), s32[]{:S(2)}) async-start(), calls=%async_computation.6 | async-start | bytes 17301504 | tf_op jit(solution)/shard_map/all_gather | solution.py:18
  44.0 538.2 %reduce-scatter.2.cloned.1.call-start = ((), (), s32[]{:S(2)}) async-start(), calls=%async_computation.5 | async-start | bytes 12976128 | tf_op jit(solution)/shard_map/reduce_scatter | solution.py:104
  178.4 6.0 copy-start.11
  178.4 6.6 %copy-start.12 = (bf16[1,6144,288]{1,2,0:T(8,128)(2,1)S(1)}, bf16[1,6144,288]{1,2,0:T(8,128)(2,1)}, u32[]{:S(2)}) copy-start(bf16[1,6144,288]{1,2,0:T(8,128)(2,1)} %param.24) | copy-start | bytes 10616836
  193.5 0.8 copy-start.8
  193.5 8.5 %copy-start.7 = (f32[128,8]{1,0:T(8,128)S(1)}, f32[128,8]{1,0:T(8,128)}, u32[]{:S(2)}) copy-start(f32[128,8]{1,0:T(8,128)} %get-tuple-element.141) | copy-start | bytes 12292
  193.5 8.5 %copy-start.5 = (f32[128,8]{1,0:T(8,128)S(1)}, f32[128,8]{1,0:T(8,128)}, u32[]{:S(2)}) copy-start(f32[128,8]{1,0:T(8,128)} %reduce_window_sum.11) | copy-start | bytes 12292
  193.5 8.7 %copy-start.10 = (f32[1,1,8]{2,1,0:T(1,128)S(1)}, f32[1,1,8]{2,1,0:T(1,128)}, u32[]{:S(2)}) copy-start(f32[1,1,8]{2,1,0:T(1,128)} %get-tuple-element.144) | copy-start | bytes 100
  193.5 102.1 %copy-start.4 = (bf16[128,1024]{0,1:T(8,128)(2,1)S(1)}, bf16[128,1024]{0,1:T(8,128)(2,1)}, u32[]{:S(2)}) copy-start(bf16[128,1024]{0,1:T(8,128)(2,1)} %copy.137) | copy-start | bytes 786436
  193.5 102.1 %copy-start.6 = (bf16[128,1024]{1,0:T(8,128)(2,1)S(1)}, bf16[128,1024]{1,0:T(8,128)(2,1)}, u32[]{:S(2)}) copy-start(bf16[128,1024]{1,0:T(8,128)(2,1)} %param.15) | copy-start | bytes 786436
  194.3 102.9 %copy-start.13 = (bf16[128,1024]{1,0:T(8,128)(2,1)S(1)}, bf16[128,1024]{1,0:T(8,128)(2,1)}, u32[]{:S(2)}) copy-start(bf16[128,1024]{1,0:T(8,128)(2,1)} %param.26) | copy-start | bytes 786436
  196.2 100.9 %all-to-all-start.2 = ((bf16[32,128,1,2,128]{4,1,3,2,0:T(8,128)(2,1)}), bf16[32,128,1,2,128]{4,1,3,2,0:T(8,128)(2,1)S(1)}, u32[]{:S(2)}, u32[]{:S(2)}) async-start(bf16[32,128,1,2,128]{4,1,3,2,0:T(8,128)(2,1)} %stack.2), calls=%async_computation.3 | async-start | bytes 4194304 | tf_op jit(solution)/shard_map/all_to_all | solution.py:128
  297.2 7.2 %copy-start.2 = (bf16[32,128,1,2,128]{4,1,0,3,2:T(8,128)(2,1)}, bf16[32,128,1,2,128]{4,1,0,3,2:T(8,128)(2,1)S(1)}, u32[]{:S(2)}) copy-start(bf16[32,128,1,2,128]{4,1,0,3,2:T(8,128)(2,1)S(1)} %copy.126) | copy-start | bytes 6291460
  304.3 9.5 %copy-start.3 = (bf16[32,128,1,2,128]{4,1,0,3,2:T(8,128)(2,1)S(1)}, bf16[32,128,1,2,128]{4,1,0,3,2:T(8,128)(2,1)}, u32[]{:S(2)}) copy-start(bf16[32,128,1,2,128]{4,1,0,3,2:T(8,128)(2,1)} %copy-done.2) | copy-start | bytes 6291460
  410.8 223.6 %copy-start.1 = (bf16[1,288,6144]{2,1,0:T(8,128)(2,1)S(1)}, bf16[1,288,6144]{2,1,0:T(8,128)(2,1)}, u32[]{:S(2)}) copy-start(bf16[1,288,6144]{2,1,0:T(8,128)(2,1)} %param.25) | copy-start | bytes 10616836
  410.8 206.3 %copy-start.9 = (f32[1024]{0:T(1024)S(1)}, f32[1024]{0:T(1024)}, u32[]{:S(2)}) copy-start(f32[1024]{0:T(1024)} %param.19) | copy-start | bytes 12292
  588.5 37.4 %all-to-all-start.1 = ((bf16[8,2,6144]{2,1,0:T(2,128)(2,1)}), bf16[8,2,6144]{2,1,0:T(2,128)(2,1)}, u32[]{:S(2)}, u32[]{:S(2)}) async-start(bf16[8,2,6144]{2,1,0:T(2,128)(2,1)} %reshape.225), calls=%async_computation.2 | async-start | bytes 393216 | tf_op jit(solution)/shard_map/all_to_all | solution.py:110
Sparse Core Ops, SparseCore 0:
  33.4 144.9 all-gather.4
  180.2 230.6 all-gather.6
  413.4 168.7 reduce-scatter.1
